TPU v7x, 128 devices: a whole 4x4x4 slice. The times are simulated.
128 devices in a mesh: dp: 4 (over x_lo, core), comp: 32 (over z, x_hi, y).
Axes of the slice: x: 4 (x_hi: 2, x_lo: 2; x = x_hi * 2 + x_lo), y: 4, z: 4, core: 2. Of those that a mesh axis runs over, the one named last changes fastest.
Arguments:
- embeddings: bfloat16 [12288, 1024], P(('dp', 'comp')), may hold values from -64 to 64
- centroids: bfloat16 [65536, 1024], P('comp'), may hold values from -64 to 64
Outputs:
- new_centroids: bfloat16 [65536, 1024], P('comp', 'dp')
- soft_counts: float32 [65536], P('comp')
- log_totals: float32 [12288], P(('dp', 'comp'))
All inputs are finite; a program needn't handle non-finite values.
Results may differ from a plain program's by a relative error of at most 0.0034.
Values may be sent and summed in bfloat16 or wider, within the bound.
A program may use at most 128 MiB of HBM per device.

v0:
```python
import jax
import jax.numpy as jnp
from jax import lax
from jax.sharding import PartitionSpec as P


def unit_rows(values):
    floats = values.astype(jnp.float32)
    return (floats * lax.rsqrt(jnp.sum(floats * floats, axis=1, keepdims=True) + 1e-06)).astype(
        jnp.bfloat16
    )


def on_device(embeddings, centroids):
    centroid_unit = unit_rows(centroids)
    group_rows = lax.all_gather(unit_rows(embeddings), "comp", axis=0, tiled=True)
    shard_rows = embeddings.shape[0]
    comp_count = lax.axis_size("comp")
    block_rows = shard_rows * min(comp_count, 8)
    block_count = group_rows.shape[0] // block_rows
    local_count = centroid_unit.shape[0]
    feature_count = centroid_unit.shape[1]

    def probabilities(row_block):
        scores = lax.dot_general(
            row_block, centroid_unit, (((1,), (1,)), ((), ())), preferred_element_type=jnp.float32
        )
        return jnp.exp(scores * 10.0 - 10.0)

    def accumulate(running, row_block, probs, totals):
        weighted, counts = running
        weights = (probs / totals[:, None]).astype(jnp.bfloat16)
        weighted = weighted + lax.dot_general(
            weights, row_block, (((0,), (0,)), ((), ())), preferred_element_type=jnp.float32
        )
        counts = counts + jnp.sum(weights.astype(jnp.float32), axis=0)
        return (weighted, counts)

    start = (
        jnp.zeros((local_count, feature_count), jnp.float32),
        jnp.zeros((local_count,), jnp.float32),
    )
    log_start = jnp.zeros((group_rows.shape[0],), jnp.float32)

    def block_step(step_index, state):
        running, log_all = state
        offset = step_index * block_rows
        row_block = lax.dynamic_slice_in_dim(group_rows, offset, block_rows, 0)
        probs = probabilities(row_block)
        totals = lax.psum(jnp.sum(probs, axis=1), "comp")
        running = accumulate(running, row_block, probs, totals)
        log_all = lax.dynamic_update_slice_in_dim(log_all, jnp.log(totals) + 10.0, offset, 0)
        return (running, log_all)

    running, log_all = lax.fori_loop(0, block_count, block_step, (start, log_start))
    weighted, counts = running
    column_count = feature_count // lax.axis_size("dp")
    weighted_all, counts_all = lax.psum((weighted, counts), "dp")
    squares = jnp.sum(weighted_all * weighted_all, axis=1, keepdims=True)
    unit_all = weighted_all * lax.rsqrt(squares + 1e-06)
    new_centroids = lax.dynamic_slice_in_dim(
        unit_all, lax.axis_index("dp") * column_count, column_count, 1
    ).astype(jnp.bfloat16)
    log_totals = lax.dynamic_slice_in_dim(
        log_all, lax.axis_index("comp") * shard_rows, shard_rows, 0
    )
    return (new_centroids, counts_all, log_totals)


def solution(mesh):
    placed = (P(("dp", "comp"), None), P("comp", None))
    return jax.shard_map(
        on_device,
        mesh=mesh,
        in_specs=placed,
        out_specs=(P("comp", "dp"), P("comp"), P(("dp", "comp"))),
        check_vma=False,
    )
```

profile of v0, /device:TPU:1, one launch (start us, length us, event | category | flops | bytes accessed | tf_op | source)
XLA Modules:
  0.0 720.0 jit_solution(11354553374563755630)
XLA Ops:
  7.2 1.1 fusion.9
  8.3 1.7 fusion.10
  10.1 3.2 fusion.6
  13.4 0.2 copy-done
  13.6 2.7 fusion.7
  16.3 90.0 %all-gather.2.cloned.1.call-done = bf16[3072,1024]{1,0:T(8,128)(2,1)} async-done(((bf16[96,1024]{1,0:T(8,128)(2,1)}), bf16[3072,1024]{1,0:T(8,128)(2,1)}) %all-gather.2.cloned.1.call-update) | async-done | bytes 6291472 | tf_op jit(solution)/shard_map/all_gather | solution.py:16
  106.3 388.5 %while.20 = (s32[]{:T(128)}, f32[2048,1024]{1,0:T(8,128)}, f32[2048]{0:T(1024)S(1)}, f32[3072]{0:T(1024)S(1)}, bf16[3072,1024]{1,0:T(8,128)(2,1)}, /*index=5*/bf...) while((s32[]{:T(128)}, f32[2048,1024]{1,0:T(8,128)}, f32[2048]{0:T(1024)S(1)}, ...), condition=%wide.region_6.0_spmd.clone, body=%wide.region_2.0_spmd.clone.sunk | while | flops 6460804096 | bytes 43045040 | solution.py:55
  106.3 8.9 %fusion.20 = (f32[768]{0:T(1024)S(1)}, f32[768,2048]{1,0:T(8,128)}) fusion(bf16[2048,1024]{1,0:T(8,128)(2,1)} %get-tuple-element.269, bf16[3072,1024]{1,0:T(8,128)(2,1)} %get-tuple-element.268, s32[]{:T(128)S(6)} %select_n.21), kind=kOutput, calls=%fused_computation.4.clone.1 | convolution fusion | flops 3225943296 | bytes 12061700 | tf_op jit(solution)/shard_map/while/body/eval_jaxpr/dot_general | solution.py:25
  115.2 77.8 %psum.32 = f32[768]{0:T(1024)S(1)} all-reduce(f32[768]{0:T(1024)S(1)} %get-tuple-element.240), channel_id=1, replica_groups=mesh['dp'=4,'comp'=32] {'comp'}, use_global_device_ids=true, to_apply=%region_4.0 | all-reduce | flops 768 | bytes 6144 | tf_op jit(solution)/shard_map/while/body/eval_jaxpr/psum | solution.py:50
  193.1 3.7 convert_reduce_fusion.2
  196.8 0.1 add_dynamic-update-slice_fusion.2
  196.9 7.2 select_add_fusion.4
  204.1 8.9 %fusion.20 = (f32[768]{0:T(1024)S(1)}, f32[768,2048]{1,0:T(8,128)}) fusion(bf16[2048,1024]{1,0:T(8,128)(2,1)} %get-tuple-element.269, bf16[3072,1024]{1,0:T(8,128)(2,1)} %get-tuple-element.268, s32[]{:T(128)S(6)} %select_n.21), kind=kOutput, calls=%fused_computation.4.clone.1 | convolution fusion | flops 3225943296 | bytes 12061700 | tf_op jit(solution)/shard_map/while/body/eval_jaxpr/dot_general | solution.py:25
  213.0 75.1 %psum.32 = f32[768]{0:T(1024)S(1)} all-reduce(f32[768]{0:T(1024)S(1)} %get-tuple-element.240), channel_id=1, replica_groups=mesh['dp'=4,'comp'=32] {'comp'}, use_global_device_ids=true, to_apply=%region_4.0 | all-reduce | flops 768 | bytes 6144 | tf_op jit(solution)/shard_map/while/body/eval_jaxpr/psum | solution.py:50
  288.1 3.7 convert_reduce_fusion.2
  291.8 0.1 add_dynamic-update-slice_fusion.2
  291.9 8.4 %select_add_fusion.4 = f32[2048,1024]{1,0:T(8,128)} fusion(f32[2048,1024]{1,0:T(8,128)} %get-tuple-element.255, pred[]{:T(512)S(6)} %compare.3, bf16[768,2048]{1,0:T(8,128)(2,1)S(1)} %get-tuple-element.242, bf16[3072,1024]{1,0:T(8,128)(2,1)} %get-tuple-element.268, s32[]{:T(128)S(6)} %select_n.21), kind=kOutput, calls=%fused_computation.clone.1 | convolution fusion | flops 3225419776 | bytes 21495812 | tf_op jit(solution)/shard_map/while/body/eval_jaxpr/dot_general | solution.py:33
  300.3 8.9 %fusion.20 = (f32[768]{0:T(1024)S(1)}, f32[768,2048]{1,0:T(8,128)}) fusion(bf16[2048,1024]{1,0:T(8,128)(2,1)} %get-tuple-element.269, bf16[3072,1024]{1,0:T(8,128)(2,1)} %get-tuple-element.268, s32[]{:T(128)S(6)} %select_n.21), kind=kOutput, calls=%fused_computation.4.clone.1 | convolution fusion | flops 3225943296 | bytes 12061700 | tf_op jit(solution)/shard_map/while/body/eval_jaxpr/dot_general | solution.py:25
  309.3 77.1 %psum.32 = f32[768]{0:T(1024)S(1)} all-reduce(f32[768]{0:T(1024)S(1)} %get-tuple-element.240), channel_id=1, replica_groups=mesh['dp'=4,'comp'=32] {'comp'}, use_global_device_ids=true, to_apply=%region_4.0 | all-reduce | flops 768 | bytes 6144 | tf_op jit(solution)/shard_map/while/body/eval_jaxpr/psum | solution.py:50
  386.3 3.7 convert_reduce_fusion.2
  390.0 0.1 add_dynamic-update-slice_fusion.2
  390.1 8.4 %select_add_fusion.4 = f32[2048,1024]{1,0:T(8,128)} fusion(f32[2048,1024]{1,0:T(8,128)} %get-tuple-element.255, pred[]{:T(512)S(6)} %compare.3, bf16[768,2048]{1,0:T(8,128)(2,1)S(1)} %get-tuple-element.242, bf16[3072,1024]{1,0:T(8,128)(2,1)} %get-tuple-element.268, s32[]{:T(128)S(6)} %select_n.21), kind=kOutput, calls=%fused_computation.clone.1 | convolution fusion | flops 3225419776 | bytes 21495812 | tf_op jit(solution)/shard_map/while/body/eval_jaxpr/dot_general | solution.py:33
  398.6 8.9 %fusion.20 = (f32[768]{0:T(1024)S(1)}, f32[768,2048]{1,0:T(8,128)}) fusion(bf16[2048,1024]{1,0:T(8,128)(2,1)} %get-tuple-element.269, bf16[3072,1024]{1,0:T(8,128)(2,1)} %get-tuple-element.268, s32[]{:T(128)S(6)} %select_n.21), kind=kOutput, calls=%fused_computation.4.clone.1 | convolution fusion | flops 3225943296 | bytes 12061700 | tf_op jit(solution)/shard_map/while/body/eval_jaxpr/dot_general | solution.py:25
  407.5 75.1 %psum.32 = f32[768]{0:T(1024)S(1)} all-reduce(f32[768]{0:T(1024)S(1)} %get-tuple-element.240), channel_id=1, replica_groups=mesh['dp'=4,'comp'=32] {'comp'}, use_global_device_ids=true, to_apply=%region_4.0 | all-reduce | flops 768 | bytes 6144 | tf_op jit(solution)/shard_map/while/body/eval_jaxpr/psum | solution.py:50
  482.6 3.7 convert_reduce_fusion.2
  486.3 0.1 add_dynamic-update-slice_fusion.2
  486.4 8.4 %select_add_fusion.4 = f32[2048,1024]{1,0:T(8,128)} fusion(f32[2048,1024]{1,0:T(8,128)} %get-tuple-element.255, pred[]{:T(512)S(6)} %compare.3, bf16[768,2048]{1,0:T(8,128)(2,1)S(1)} %get-tuple-element.242, bf16[3072,1024]{1,0:T(8,128)(2,1)} %get-tuple-element.268, s32[]{:T(128)S(6)} %select_n.21), kind=kOutput, calls=%fused_computation.clone.1 | convolution fusion | flops 3225419776 | bytes 21495812 | tf_op jit(solution)/shard_map/while/body/eval_jaxpr/dot_general | solution.py:33
  494.9 0.6 dynamic_slice.17
  495.5 62.2 %psum.29 = f32[2048]{0:T(1024)} all-reduce(f32[2048]{0:T(1024)S(1)} %get-tuple-element.160), channel_id=1, replica_groups=mesh['dp'=4,'comp'=32] {'dp'}, use_global_device_ids=true, to_apply=%region_9.0 | all-reduce | flops 2048 | bytes 16384 | tf_op jit(solution)/shard_map/psum | solution.py:58
  557.7 148.6 %all-reduce.2.cloned.1.call-done = f32[2048,1024]{1,0:T(8,128)} async-done(((f32[2048,1024]{1,0:T(8,128)}), f32[2048,1024]{1,0:T(8,128)}) %all-reduce.2.cloned.1.call-update) | async-done | bytes 8388624 | tf_op jit(solution)/shard_map/psum | solution.py:58
  706.3 4.0 multiply_reduce_fusion
  710.3 2.9 fusion.8
  (15 shorter events, 0.2 us)
Async XLA Ops:
  7.2 99.1 %all-gather.2.cloned.1.call-start = ((), (), s32[]{:S(2)}) async-start(), calls=%async_computation | async-start | bytes 6488064 | tf_op jit(solution)/shard_map/all_gather | solution.py:16
  10.0 696.2 %all-reduce.2.cloned.1.call-start = ((), (), s32[]{:S(2)}) async-start(), calls=%async_computation.1 | async-start | bytes 16777216 | tf_op jit(solution)/shard_map/psum | solution.py:58
  10.1 3.5 copy-start
Sparse Core Ops, SparseCore 0:
  11.6 94.6 all-gather.1
  495.0 211.2 all-reduce.1
where the time goes:
time: 720 us
  blocking collectives  367 us (51%)
  waiting for transfers between devices  239 us (33%)
  matrix products  68.2 us (9%)
  other arithmetic  30.9 us (4%)
  between operations  14.1 us (2%)
    psum x4, blocking collectives, block_step(): totals = lax.psum(jnp.sum(probs, axis=1), 'comp')  305 us
    psum x1, waiting for transfers between devices, on_device(): weighted_all, counts_all = lax.psum((weighted, counts), 'dp')  149 us
    all_gather x1, waiting for transfers between devices, on_device(): lax.all_gather(unit_rows(embeddings), 'comp', axis=0, tiled=True)  90 us
    psum x1, blocking collectives, on_device(): weighted_all, counts_all = lax.psum((weighted, counts), 'dp')  62.2 us
    dot_general x4, matrix products, probabilities(): lax.dot_general(row_block, centroid_unit, (((1,), (1,)), ((), ())), prefe...  35.7 us
    dot_general x4, matrix products, accumulate(): lax.dot_general(weights, row_block, (((0,), (0,)), ((), ())), preferred_e...  32.5 us
    reduce_sum x4, other arithmetic, accumulate(): counts = counts + jnp.sum(weights.astype(jnp.float32), axis=0)  14.7 us
  transfers between devices with their start and end apart: 2, of which 2 were waited for; matrix products, arithmetic and copies ran while one was open for 1% of the time, Pallas kernels for 0%

commit v1 on v0

v1 whole, which is shorter than its diff:
```python
import jax
import jax.numpy as jnp
from jax import lax
from jax.experimental import pallas as pl
from jax.experimental.pallas import tpu as pltpu
from jax.sharding import PartitionSpec as P

MESH = pl.DeviceIdType.MESH
F32 = jnp.float32
BF16 = jnp.bfloat16

ORDER = (
    (0, 0), (1, 0), (0, 1), (3, 0), (0, 3), (2, 0), (0, 2), (1, 1),
    (3, 3), (1, 3), (3, 1), (2, 1), (1, 2), (2, 3), (3, 2), (2, 2),
)
SLOTS = len(ORDER)
SLOT_OF = {place: slot for slot, place in enumerate(ORDER)}
NODE = 128
HALF = NODE // 2
STEP = 2 * NODE
BATCH = SLOTS * STEP
ROWS_A = 64
ROWS_B = 32
NEXT_BATCH_AT = 12


def children(slot, half):
    place = ORDER[slot]
    first, second = place if half == 0 else place[::-1]
    found = []
    if second == 0:
        if first == 0:
            found += [((1, 0), 0, 1), ((3, 0), 0, -1)]
        if first == 1:
            found += [((2, 0), 0, 1)]
        found += [((first, 1), 1, 1), ((first, 3), 1, -1)]
    elif second == 1 and first in (0, 1):
        found += [((first, 2), 1, 1)]
    elif second == 3 and first in (2, 3):
        found += [((first, 2), 1, -1)]
    if half == 0:
        return [(SLOT_OF[p], axis, way) for p, axis, way in found]
    return [(SLOT_OF[p[::-1]], 1 - axis, way) for p, axis, way in found]


def kernel(
    emb_hbm, cent_hbm, out_hbm, count_out, log_out,
    rows, probs, cent, emb, own_sum, sum_send, sum_recv, final,
    part_src, part_dst, x_src, x_dst, inv, inv_src, count, count_src, count_dst, count_all, sq_src, sq_dst,
    load_sem, row_send, row_recv, sib_send, sib_recv, pre_send, pre_recv,
    part_send, part_recv, xs_send, xs_recv, inv_send, inv_recv,
    sum_ssem, sum_rsem, cnt_send, cnt_recv, sq_send, sq_recv, out_sem, out_send, out_recv, all_send, all_recv,
):
    dp = lax.axis_index("dp")
    comp = lax.axis_index("comp")
    core = lax.rem(dp, 2)
    other = 1 - core
    x_lo = dp // 2
    y = lax.rem(comp, 4)
    x = lax.rem(comp // 4, 2) * 2 + x_lo
    z = comp // 8
    sign = 1 - 2 * core

    def device(dx, dy, dz, dcore):
        nx = lax.rem(x + dx + 4, 4)
        ny = lax.rem(y + dy + 4, 4)
        nz = lax.rem(z + dz + 4, 4)
        ncore = lax.rem(core + dcore, 2)
        return {"dp": lax.rem(nx, 2) * 2 + ncore, "comp": nz * 8 + (nx // 2) * 4 + ny}

    def remote(src, dst, ssem, rsem, target):
        return pltpu.make_async_remote_copy(
            src_ref=src, dst_ref=dst, send_sem=ssem, recv_sem=rsem, device_id=target, device_id_type=MESH
        )

    def wait_bytes(ref, sem):
        pltpu.make_async_copy(ref, ref, sem).wait()

    sibling = device(0, 0, 0, 1)
    x_far = device(2, 0, 0, 0)
    x_pair = device(1 - 2 * x_lo, 0, 0, 0)

    barrier = pltpu.get_barrier_semaphore()
    greeted = 0
    for dy, dz in ORDER:
        for dcore in (0, 1):
            if (dy, dz, dcore) != (0, 0, 0):
                pl.semaphore_signal(barrier, inc=1, device_id=device(0, dy, dz, dcore), device_id_type=MESH)
                greeted += 1
    for dx in (1, 2, 3):
        pl.semaphore_signal(barrier, inc=1, device_id=device(dx, 0, 0, 0), device_id_type=MESH)
        greeted += 1

    emb_copy = pltpu.make_async_copy(emb_hbm, emb, load_sem.at[0])
    emb_copy.start()
    cent_copy = pltpu.make_async_copy(cent_hbm.at[pl.ds(core * 1024, 1024)], cent, load_sem.at[1])
    cent_copy.start()

    def unit(values):
        floats = values.astype(F32)
        return (floats * lax.rsqrt(jnp.sum(floats * floats, axis=1, keepdims=True) + 1e-06)).astype(BF16)

    emb_copy.wait()
    rows[0, pl.ds(0, ROWS_A), :] = unit(emb[pl.ds(0, ROWS_A), :])
    rows[1, pl.ds(0, ROWS_B), :] = unit(emb[pl.ds(ROWS_A, ROWS_B), :])
    pl.semaphore_wait(barrier, greeted)

    def pre(batch, size, chunk, dx):
        return remote(
            rows.at[batch, pl.ds(0, size)],
            rows.at[batch, pl.ds(chunk * size, size)],
            pre_send.at[batch, chunk],
            pre_recv.at[batch, chunk],
            device(-dx, 0, 0, 0),
        )

    pres = [pre(0, ROWS_A, 1, 2)] + [pre(1, ROWS_B, j, j) for j in (1, 2, 3)]
    pres[0].start()

    def row_copy(batch, slot, half, child, axis, way):
        dy, dz = (way * sign, 0) if axis == 0 else (0, way * sign)
        return remote(
            rows.at[batch, pl.ds(slot * STEP + half * HALF, HALF)],
            rows.at[batch, pl.ds(child * STEP + half * HALF, HALF)],
            row_send.at[batch],
            row_recv.at[batch, child, half],
            device(0, dy, dz, 0),
        )

    def hand_on(batch, slot, half):
        for child, axis, way in children(slot, half):
            row_copy(batch, slot, half, child, axis, way).start()

    def to_sibling(batch, slot):
        return remote(
            rows.at[batch, pl.ds(slot * STEP, NODE)],
            rows.at[batch, pl.ds(slot * STEP + NODE, NODE)],
            sib_send.at[batch],
            sib_recv.at[batch, slot],
            sibling,
        )

    def arrive(batch, slot):
        for half in (0, 1):
            row_copy(batch, slot, half, slot, 0, 1).wait_recv()
            hand_on(batch, slot, half)
        to_sibling(batch, slot).start()

    hand_on(0, 0, 0)
    for copy in pres[1:]:
        copy.start()
    pres[0].wait_recv()
    hand_on(0, 0, 1)
    to_sibling(0, 0).start()

    cent_copy.wait()

    def unit_block(i, carry):
        block = pl.ds(i * 128, 128)
        cent[block, :] = unit(cent[block, :])
        return carry

    lax.fori_loop(0, 8, unit_block, 0)
    for copy in pres[1:]:
        copy.wait_recv()

    def score(batch, slot):
        block = rows[batch, pl.ds(slot * STEP, STEP), :]
        scores = lax.dot_general(cent[...], block, (((1,), (1,)), ((), ())), preferred_element_type=F32)
        p = jnp.exp(scores * 10.0 - 10.0)
        probs[batch, :, pl.ds(slot * STEP, STEP)] = p.astype(BF16)
        part = jnp.sum(p.reshape(128, 8, STEP), axis=0)
        part_src[batch, 2 * slot] = part[:, :NODE]
        part_src[batch, 2 * slot + 1] = part[:, NODE:]

    def send_part(batch, slot):
        dy, dz = ORDER[slot]
        if slot > 0:
            remote(
                part_src.at[batch, 2 * slot], part_dst.at[batch, 2 * slot], part_send.at[batch], part_recv.at[batch],
                device(0, -sign * dy, -sign * dz, 0),
            ).start()
        else:
            part_dst[batch, 0] = part_src[batch, 0]
        remote(
            part_src.at[batch, 2 * slot + 1], part_dst.at[batch, 2 * slot + 1], part_send.at[batch], part_recv.at[batch],
            device(0, sign * dy, sign * dz, 1),
        ).start()

    def x_copy(batch):
        return remote(x_src.at[batch], x_dst.at[batch], xs_send.at[batch], xs_recv.at[batch], x_far)

    def totals_first(batch):
        wait_bytes(part_dst.at[batch, pl.ds(1, 2 * SLOTS - 1)], part_recv.at[batch])
        x_src[batch] = jnp.sum(part_dst[batch], axis=0)
        x_copy(batch).start()

    def totals_second(batch):
        x_copy(batch).wait_recv()
        tile = x_src[batch] + pltpu.roll(x_dst[batch], HALF, 1)
        total = jnp.broadcast_to(jnp.sum(tile, axis=0, keepdims=True), (8, NODE))
        inv_src[batch] = 1.0 / total
        inv[batch, 0] = 1.0 / total
        for slot, (dy, dz) in enumerate(ORDER):
            for dcore in (0, 1):
                if slot + dcore > 0:
                    remote(
                        inv_src.at[batch], inv.at[batch, 2 * slot + dcore], inv_send.at[batch], inv_recv.at[batch],
                        device(0, sign * dy, sign * dz, dcore),
                    ).start()
        return jnp.log(total) + 10.0

    def totals_third(batch):
        wait_bytes(inv.at[batch, pl.ds(1, 2 * SLOTS - 1)], inv_recv.at[batch])

    def scale(batch, m):
        def block(i, carry):
            at = pl.ds(m * 512 + i * 64, 64)
            total = jnp.zeros((64, NODE), F32)
            for tile in range(2 * SLOTS):
                lanes = pl.ds(tile * NODE, NODE)
                weights = (probs[batch, at, lanes].astype(F32) * inv[batch, tile, 0:1, :]).astype(BF16)
                probs[batch, at, lanes] = weights
                total = total + weights.astype(F32)
            count[at, :] = total
            return carry

        lax.fori_loop(0, 8, block, 0)

    def to_row(block):
        return jnp.sum(block.T, axis=0, keepdims=True)

    def weighted(batch, m, column):
        return lax.dot_general(
            probs[batch, pl.ds(m * 512, 512), :],
            rows[batch, :, pl.ds(column, 512)],
            (((1,), (0,)), ((), ())),
            preferred_element_type=F32,
        )

    def sum_copy(m):
        at = pl.ds(m * 512, 512)
        return remote(sum_send.at[at], sum_recv.at[at], sum_ssem.at[m], sum_rsem.at[m], x_pair)

    def count_copy():
        return remote(count_src.at[0], count_dst, cnt_send, cnt_recv, x_pair)

    def count_rows(batch, m):
        def one(i, carry):
            r = m * 4 + i
            count_src[batch, pl.ds(r, 1), :] = to_row(count[pl.ds(r * 128, 128), :])
            return carry

        lax.fori_loop(0, 4, one, 0)

    def step(t, carry):
        batch = t // SLOTS
        slot = lax.rem(t, SLOTS)
        ahead = (t + 1) // SLOTS
        for k in range(1, SLOTS):
            @pl.when(lax.rem(t + 1, SLOTS) == k)
            def _():
                arrive(ahead, k)

        @pl.when(t == NEXT_BATCH_AT)
        def _():
            hand_on(1, 0, 0)
            hand_on(1, 0, 1)
            to_sibling(1, 0).start()

        to_sibling(batch, slot).wait_recv()
        score(batch, slot)
        for k in range(SLOTS):
            @pl.when(slot == k)
            def _():
                send_part(batch, k)

        @pl.when(t == SLOTS)
        def _():
            totals_first(0)

        @pl.when(t == SLOTS + 1)
        def _():
            logs = totals_second(0)
            log_out[0:1, :] = logs[0:1]

        @pl.when(t == SLOTS + 3)
        def _():
            totals_third(0)

        @pl.when((t == SLOTS + 3) | (t == SLOTS + 4))
        def _():
            m = t - (SLOTS + 3)
            scale(0, m)
            at = pl.ds(m * 512, 512)
            sum_send[at, :] = weighted(0, m, (1 - x_lo) * 512).astype(BF16)
            sum_copy(m).start()
            count_rows(0, m)

        @pl.when(t == SLOTS + 5)
        def _():
            count_copy().start()

        @pl.when((t == SLOTS + 6) | (t == SLOTS + 8))
        def _():
            m = (t - (SLOTS + 6)) // 2
            own_sum[pl.ds(m * 512, 512), :] = weighted(0, m, x_lo * 512)

        return carry

    lax.fori_loop(0, 2 * SLOTS, step, 0)

    totals_first(1)
    logs = totals_second(1)
    log_out[1:2, :] = logs[0:1]
    totals_third(1)

    def sq_copy(m):
        return remote(sq_src.at[m], sq_dst.at[m], sq_send.at[m], sq_recv.at[m], x_pair)

    def finish(m, carry):
        at = pl.ds(m * 512, 512)
        scale(1, m)
        total = weighted(1, m, x_lo * 512) + own_sum[at, :]
        sum_copy(m).wait_recv()
        total = total + sum_recv[at, :].astype(F32)
        own_sum[at, :] = total
        squares = total * total
        lanes = squares[:, :128] + squares[:, 128:256] + squares[:, 256:384] + squares[:, 384:]
        sq_src[m] = jnp.concatenate(
            [to_row(lanes[i * 128 : (i + 1) * 128]) for i in range(4)] + [jnp.zeros((4, 128), F32)], axis=0
        )
        sq_copy(m).start()
        count_rows(1, m)
        return carry

    lax.fori_loop(0, 2, finish, 0)

    count_copy().wait_recv()
    mine = pl.ds(pl.multiple_of(core * 8, 8), 8)
    count_all[mine, :] = count_src[0] + count_dst[...] + count_src[1]
    all_copy = remote(count_all.at[mine], count_all.at[mine], all_send, all_recv, sibling)
    all_copy.start()

    def out_copies(m):
        at = pl.ds(m * 512, 512)
        place = pl.ds(core * 1024 + m * 512, 512)
        local = pltpu.make_async_copy(
            final.at[at, pl.ds(pl.multiple_of(core * 256, 256), 256)], out_hbm.at[place], out_sem.at[m]
        )
        away = remote(
            final.at[at, pl.ds(pl.multiple_of(other * 256, 256), 256)],
            out_hbm.at[place],
            out_send.at[m],
            out_recv.at[m],
            sibling,
        )
        return local, away

    def normalize(m, carry):
        sq_copy(m).wait_recv()

        def one(i, carry):
            at = pl.ds(m * 512 + i * 128, 128)
            squares = sq_src[m, pl.ds(i, 1), :] + sq_dst[m, pl.ds(i, 1), :]
            factor = jnp.broadcast_to(lax.rsqrt(squares + 1e-06), (128, 128)).T
            for tile in range(4):
                lanes = pl.ds(tile * 128, 128)
                final[at, lanes] = (own_sum[at, lanes] * factor).astype(BF16)
            return carry

        lax.fori_loop(0, 4, one, 0)
        local, away = out_copies(m)
        local.start()
        away.start()
        return carry

    lax.fori_loop(0, 2, normalize, 0)

    all_copy.wait()
    count_out[...] = count_all[...]
    for copy in pres:
        copy.wait_send()
    for batch in (0, 1):
        wait_bytes(rows.at[batch, pl.ds(0, (SLOTS - 1) * NODE)], row_send.at[batch])
        wait_bytes(rows.at[batch, pl.ds(0, SLOTS * NODE)], sib_send.at[batch])
        wait_bytes(part_dst.at[batch, pl.ds(1, 2 * SLOTS - 1)], part_send.at[batch])
        wait_bytes(inv.at[batch, pl.ds(1, 2 * SLOTS - 1)], inv_send.at[batch])
        x_copy(batch).wait_send()
    count_copy().wait_send()
    for m in (0, 1):
        sum_copy(m).wait_send()
        sq_copy(m).wait_send()
        local, away = out_copies(m)
        local.wait()
        away.wait()


def on_device(embeddings, centroids):
    dma = pltpu.SemaphoreType.DMA
    any_space = pl.BlockSpec(memory_space=pl.ANY)
    vmem = pl.BlockSpec(memory_space=pltpu.VMEM)
    new_centroids, counts, logs = pl.pallas_call(
        kernel,
        out_shape=(
            jax.ShapeDtypeStruct((2048, 256), BF16),
            jax.ShapeDtypeStruct((16, 128), F32),
            jax.ShapeDtypeStruct((2, 128), F32),
        ),
        in_specs=[any_space, any_space],
        out_specs=(any_space, vmem, vmem),
        scratch_shapes=[
            pltpu.VMEM((2, BATCH, 1024), BF16),
            pltpu.VMEM((2, 1024, BATCH), BF16),
            pltpu.VMEM((1024, 1024), BF16),
            pltpu.VMEM((96, 1024), BF16),
            pltpu.VMEM((1024, 512), F32),
            pltpu.VMEM((1024, 512), BF16),
            pltpu.VMEM((1024, 512), BF16),
            pltpu.VMEM((1024, 512), BF16),
            pltpu.VMEM((2, 2 * SLOTS, 8, NODE), F32),
            pltpu.VMEM((2, 2 * SLOTS, 8, NODE), F32),
            pltpu.VMEM((2, 8, NODE), F32),
            pltpu.VMEM((2, 8, NODE), F32),
            pltpu.VMEM((2, 2 * SLOTS, 8, NODE), F32),
            pltpu.VMEM((2, 8, NODE), F32),
            pltpu.VMEM((1024, NODE), F32),
            pltpu.VMEM((2, 8, 128), F32),
            pltpu.VMEM((8, 128), F32),
            pltpu.VMEM((16, 128), F32),
            pltpu.VMEM((2, 8, 128), F32),
            pltpu.VMEM((2, 8, 128), F32),
            dma((2,)),
            dma((2,)), dma((2, SLOTS, 2)),
            dma((2,)), dma((2, SLOTS)),
            dma((2, 4)), dma((2, 4)),
            dma((2,)), dma((2,)),
            dma((2,)), dma((2,)),
            dma((2,)), dma((2,)),
            dma((2,)), dma((2,)),
            dma, dma,
            dma((2,)), dma((2,)),
            dma((2,)), dma((2,)), dma((2,)),
            dma, dma,
        ],
        compiler_params=pltpu.CompilerParams(
            collective_id=0, has_side_effects=True, vmem_limit_bytes=60 * 1024 * 1024
        ),
        name="soft_kmeans",
    )(embeddings, centroids)
    log_totals = jnp.concatenate([logs[0, :ROWS_A], logs[1, :ROWS_B]])
    return new_centroids, counts.reshape(2048), log_totals


def solution(mesh):
    return jax.shard_map(
        on_device,
        mesh=mesh,
        in_specs=(P(("dp", "comp"), None), P("comp", None)),
        out_specs=(P("comp", "dp"), P("comp"), P(("dp", "comp"))),
        check_vma=False,
    )
```

time: 720 us -> 131 us (0.18)
  blocking collectives: 367 us -> 0 us
  waiting for transfers between devices: 239 us -> 0 us
  Pallas kernels: 0 us -> 124 us
  matrix products: 68.2 us -> 0 us
  other arithmetic: 30.9 us -> 0.59 us
  between operations: 14.1 us -> 0.64 us
    psum x5 -> x0, blocking collectives: 367 us -> none  [the longest x4 305 us: block_step(): totals = lax.psum(jnp.sum(probs, axis=1), 'comp')]
    psum x1 -> x0, waiting for transfers between devices: 149 us -> none  [on_device(): weighted_all, counts_all = lax.psum((weighted, counts), 'dp')]
    pallas_call x0 -> x1, Pallas kernels: none -> 124 us  [on_device(): pl.pallas_call(kernel, out_shape=(jax.ShapeDtypeStruct((2048, 256), BF16)...]
    all_gather x1 -> x0, waiting for transfers between devices: 90 us -> none  [on_device(): lax.all_gather(unit_rows(embeddings), 'comp', axis=0, tiled=True)]
    dot_general x8 -> x0, matrix products: 68.2 us -> none  [the longest x4 35.7 us: probabilities(): lax.dot_general(row_block, centroid_unit, (((1,), (1,)), ((), ())), prefe...]
    reduce_sum x7 -> x0, other arithmetic: 23 us -> none  [the longest x4 14.7 us: accumulate(): counts = counts + jnp.sum(weights.astype(jnp.float32), axis=0)]
    convert_element_type x3 -> x0, other arithmetic: 7.33 us -> none  [the longest x2 4.42 us: unit_rows(): (floats * lax.rsqrt(jnp.sum(floats * floats, axis=1, keepdims=True) + 1e-...]
  transfers between devices with their start and end apart: 2 -> 0, of which waited for: 2 -> 0; matrix products, arithmetic and copies ran while one was open for 1% -> 0% of each run, Pallas kernels for 0% -> 0%
where the time goes in v1:
time: 131 us
  Pallas kernels  124 us (95%)
  local copies, waits for them, and re-layouts  4.87 us (4%)
    pallas_call x1, Pallas kernels, on_device(): pl.pallas_call(kernel, out_shape=(jax.ShapeDtypeStruct((2048, 256), BF16)...  124 us
    unnamed x2, local copies, waits for them, and re-layouts  3.56 us

profile of v1, /device:TPU:1, one launch (start us, length us, event | category | flops | bytes accessed | tf_op | source)
XLA Modules:
  0.0 130.5 jit_solution(14722906263581387532)
XLA Ops:
  0.6 124.4 %soft_kmeans.1 = (bf16[2048,256]{1,0:T(8,128)(2,1)}, f32[16,128]{1,0:T(8,128)}, f32[2,128]{1,0:T(2,128)}) custom-call(bf16[96,1024]{1,0:T(8,128)(2,1)} %emb_hbm.1, bf16[2048,1024]{1,0:T(8,128)(2,1)} %cent_hbm.1), custom_call_target="tpu_custom_call" | custom-call | tf_op jit(solution)/shard_map/soft_kmeans/pallas_call | solution.py:403
  125.1 0.7 slice_bitcast_fusion
  125.7 0.7 slice_bitcast_fusion.1
  126.4 0.6 pad_maximum_fusion
  127.0 2.3 %copy.7 = bf16[2048,256]{1,0:T(8,128)(2,1)} copy(bf16[2048,256]{1,0:T(8,128)(2,1)} %get-tuple-element.12) | data formatting | bytes 2097152
  129.2 1.3 copy.8

commit v2 on v0

v2 whole, which is shorter than its diff:
```python
import jax
import jax.numpy as jnp
from jax import lax
from jax.experimental import pallas as pl
from jax.experimental.pallas import tpu as pltpu
from jax.sharding import PartitionSpec as P

MESH = pl.DeviceIdType.MESH
F32 = jnp.float32
BF16 = jnp.bfloat16

ORDER = (
    (0, 0), (1, 0), (0, 1), (3, 0), (0, 3), (2, 0), (0, 2), (1, 1),
    (3, 3), (1, 3), (3, 1), (2, 1), (1, 2), (2, 3), (3, 2), (2, 2),
)
SLOTS = len(ORDER)
SLOT_OF = {place: slot for slot, place in enumerate(ORDER)}
OWN = 96
EARLY = 64
NODE = 2 * OWN
HALF = (OWN + EARLY) // 2
STEP = 2 * NODE
ROWS = SLOTS * STEP
LEAD = 2
PART = 256
LUMP = 256
LUMPS = 1024 // LUMP


def children(slot, half):
    place = ORDER[slot]
    first, second = place if half == 0 else place[::-1]
    found = []
    if second == 0:
        if first == 0:
            found += [((1, 0), 0, 1), ((3, 0), 0, -1)]
        if first == 1:
            found += [((2, 0), 0, 1)]
        found += [((first, 1), 1, 1), ((first, 3), 1, -1)]
    elif second == 1 and first in (0, 1):
        found += [((first, 2), 1, 1)]
    elif second == 3 and first in (2, 3):
        found += [((first, 2), 1, -1)]
    if half == 0:
        return [(SLOT_OF[p], axis, way) for p, axis, way in found]
    return [(SLOT_OF[p[::-1]], 1 - axis, way) for p, axis, way in found]


def choose(index, low, high, work):
    if high - low == 1:
        work(low)
        return
    middle = (low + high) // 2
    pl.when(index < middle)(lambda: choose(index, low, middle, work))
    pl.when(index >= middle)(lambda: choose(index, middle, high, work))


def kernel(
    emb_hbm, cent_hbm, out_hbm, count_out, log_out,
    rows, probs, cent, emb, own_sum, sum_send, sum_recv, final,
    part_src, part_dst, inv, inv_src, inv_row, count, count_src, count_dst, count_all, sq_src, sq_dst,
    load_sem, row_send, row_recv, sib_send, sib_recv, pre_send, pre_recv, late_send, late_recv,
    part_send, part_recv, inv_send, inv_recv,
    sum_ssem, sum_rsem, cnt_send, cnt_recv, sq_send, sq_recv, out_sem, out_send, out_recv, all_send, all_recv,
):
    dp = lax.axis_index("dp")
    comp = lax.axis_index("comp")
    core = lax.rem(dp, 2)
    other = 1 - core
    x_lo = dp // 2
    y = lax.rem(comp, 4)
    x = lax.rem(comp // 4, 2) * 2 + x_lo
    z = comp // 8
    sign = 1 - 2 * core

    at_y = [lax.rem(y + sign * d + 4, 4) for d in range(4)]
    at_z = [lax.rem(z + sign * d + 4, 4) * 8 for d in range(4)]
    at_x = [lax.rem(x + d, 4) for d in range(4)]
    at_x_comp = [(place // 2) * 4 for place in at_x]
    at_x_dp = [lax.rem(place, 2) * 2 for place in at_x]
    cores = (core, other)

    def device(dx, dy, dz, dcore):
        comp_id = at_z[dz % 4] + at_x_comp[dx % 4] + at_y[dy % 4]
        return {"dp": at_x_dp[dx % 4] + cores[dcore], "comp": comp_id}

    def remote(src, dst, ssem, rsem, target):
        return pltpu.make_async_remote_copy(
            src_ref=src, dst_ref=dst, send_sem=ssem, recv_sem=rsem, device_id=target, device_id_type=MESH
        )

    def wait_bytes(ref, sem):
        pltpu.make_async_copy(ref, ref, sem).wait()

    sibling = device(0, 0, 0, 1)
    x_far = device(2, 0, 0, 0)
    x_pair = {"dp": (1 - x_lo) * 2 + core, "comp": comp}

    barrier = pltpu.get_barrier_semaphore()
    greeted = 0
    for dy, dz in ORDER:
        for dcore in (0, 1):
            if (dy, dz, dcore) != (0, 0, 0):
                pl.semaphore_signal(barrier, inc=1, device_id=device(0, dy, dz, dcore), device_id_type=MESH)
                greeted += 1
            pl.semaphore_signal(barrier, inc=1, device_id=device(2, dy, dz, dcore), device_id_type=MESH)
            greeted += 1
    for dx in (1, 3):
        pl.semaphore_signal(barrier, inc=1, device_id=device(dx, 0, 0, 0), device_id_type=MESH)
        greeted += 1

    emb_copy = pltpu.make_async_copy(emb_hbm, emb, load_sem.at[0])
    emb_copy.start()
    cent_copy = pltpu.make_async_copy(cent_hbm.at[pl.ds(core * 1024, 1024)], cent, load_sem.at[1])
    cent_copy.start()

    def unit(values):
        floats = values.astype(F32)
        return (floats * lax.rsqrt(jnp.sum(floats * floats, axis=1, keepdims=True) + 1e-06)).astype(BF16)

    emb_copy.wait()
    rows[pl.ds(0, OWN), :] = unit(emb[...])
    pl.semaphore_wait(barrier, greeted)

    pre = remote(rows.at[pl.ds(0, EARLY)], rows.at[pl.ds(OWN, EARLY)], pre_send, pre_recv, x_far)
    pre.start()

    def row_copy(slot, half, child, axis, way):
        dy, dz = (way, 0) if axis == 0 else (0, way)
        return remote(
            rows.at[pl.ds(slot * STEP + half * HALF, HALF)],
            rows.at[pl.ds(child * STEP + half * HALF, HALF)],
            row_send,
            row_recv.at[child, half],
            device(0, dy, dz, 0),
        )

    def hand_on(slot, half):
        for child, axis, way in children(slot, half):
            row_copy(slot, half, child, axis, way).start()

    def late_copy(slot):
        at = slot * STEP
        return remote(
            rows.at[pl.ds(at + EARLY, OWN - EARLY)],
            rows.at[pl.ds(at + OWN + EARLY, OWN - EARLY)],
            late_send,
            late_recv.at[slot],
            x_far,
        )

    def to_sibling(slot, late):
        first, size = (OWN + EARLY, OWN - EARLY) if late else (0, OWN + EARLY)
        at = slot * STEP + first
        return remote(
            rows.at[pl.ds(at, size)], rows.at[pl.ds(at + NODE, size)], sib_send, sib_recv.at[slot, late], sibling
        )

    def arrive(slot):
        for half in (0, 1):
            row_copy(slot, half, slot, 0, 1).wait_recv()
            hand_on(slot, half)
        late_copy(slot).start()
        to_sibling(slot, 0).start()

    hand_on(0, 0)
    pre.wait_recv()
    hand_on(0, 1)
    late_copy(0).start()
    to_sibling(0, 0).start()

    cent_copy.wait()

    def unit_block(i, carry):
        block = pl.ds(i * 128, 128)
        cent[block, :] = unit(cent[block, :])
        return carry

    lax.fori_loop(0, 8, unit_block, 0)
    def score(slot):
        at = pl.ds((slot - 1) * STEP, 2 * STEP)
        scores = lax.dot_general(cent[...], rows[at, :], (((1,), (1,)), ((), ())), preferred_element_type=F32)
        p = jnp.exp(scores * 10.0 - 10.0)
        probs[:, at] = p.astype(BF16)
        part = jnp.sum(p, axis=0, keepdims=True)
        for i in (0, 1):
            node = part[:, i * STEP : (i + 1) * STEP]
            part_src[2 * (slot - 1 + i)] = node[:, :PART]
            part_src[2 * (slot - 1 + i) + 1] = pltpu.roll(node, STEP - NODE, 1)[:, :PART]

    def send_part(slot):
        dy, dz = ORDER[slot]
        for dcore, way in ((0, -1), (1, 1)):
            tile = 2 * slot + dcore
            for dx, first in ((0, 0), (2, 2 * SLOTS)):
                if dx + tile == 0:
                    part_dst[0] = part_src[0]
                else:
                    remote(
                        part_src.at[tile], part_dst.at[first + tile], part_send, part_recv,
                        device(dx, way * dy, way * dz, dcore),
                    ).start()

    def totals_first():
        wait_bytes(part_dst.at[pl.ds(1, 4 * SLOTS - 1)], part_recv)
        near = jnp.sum(part_dst[pl.ds(0, 2 * SLOTS)], axis=0)
        far = jnp.sum(part_dst[pl.ds(2 * SLOTS, 2 * SLOTS)], axis=0)
        lane = lax.broadcasted_iota(jnp.int32, (1, PART), 1)
        total = near + jnp.where(lane < OWN, pltpu.roll(far, PART - OWN, 1), pltpu.roll(far, OWN, 1))
        total = jnp.where(lane < NODE, total, 1.0)
        inv_src[...] = 1.0 / total
        inv[0] = 1.0 / total
        for slot, (dy, dz) in enumerate(ORDER):
            for dcore in (0, 1):
                if slot + dcore > 0:
                    remote(
                        inv_src, inv.at[2 * slot + dcore], inv_send, inv_recv, device(0, dy, dz, dcore)
                    ).start()
        log_out[...] = jnp.log(total[:, :128]) + 10.0

    def totals_second():
        wait_bytes(inv.at[pl.ds(1, 2 * SLOTS - 1)], inv_recv)
        lane = lax.broadcasted_iota(jnp.int32, (1, STEP), 1)
        rest = jnp.zeros((1, STEP - PART), F32)
        for slot in range(SLOTS):
            mine = jnp.concatenate([inv[2 * slot], rest], axis=1)
            theirs = pltpu.roll(jnp.concatenate([inv[2 * slot + 1], rest], axis=1), NODE, 1)
            inv_row[:, pl.ds(slot * STEP, STEP)] = jnp.where(lane < NODE, mine, theirs)

    def scale(start, size):
        def block(i, carry):
            at = pl.ds(start + i * 64, 64)
            total = jnp.zeros((64, 128), F32)
            for tile in range(ROWS // 128):
                lanes = pl.ds(tile * 128, 128)
                weights = (probs[at, lanes].astype(F32) * inv_row[:, lanes]).astype(BF16)
                probs[at, lanes] = weights
                total = total + weights.astype(F32)
            count[at, :] = total
            return carry

        lax.fori_loop(0, size // 64, block, 0)

    def to_row(block):
        return jnp.sum(block.T, axis=0, keepdims=True)

    def weighted(start, column):
        return lax.dot_general(
            probs[pl.ds(start, LUMP), :],
            rows[:, pl.ds(column, 512)],
            (((1,), (0,)), ((), ())),
            preferred_element_type=F32,
        )

    def sum_copy(m):
        at = pl.ds(m * LUMP, LUMP)
        return remote(sum_send.at[at], sum_recv.at[at], sum_ssem.at[m], sum_rsem.at[m], x_pair)

    count_copy = remote(count_src, count_dst, cnt_send, cnt_recv, x_pair)

    def step(t, carry):
        @pl.when(t < SLOTS - LEAD)
        def _():
            choose(t + LEAD, LEAD, SLOTS, arrive)

        late_copy(t).wait_recv()
        to_sibling(t, 1).start()

        @pl.when(lax.rem(t, 2) == 1)
        def _():
            for slot in (t - 1, t):
                for late in (0, 1):
                    to_sibling(slot, late).wait_recv()
            score(t)
            choose(t // 2, 0, SLOTS // 2, lambda k: (send_part(2 * k), send_part(2 * k + 1)))

        return carry

    for slot in range(1, LEAD):
        arrive(slot)
    lax.fori_loop(0, SLOTS, step, 0)
    totals_first()
    totals_second()

    def partner_half(m, carry):
        scale(m * LUMP, LUMP)
        sum_send[pl.ds(m * LUMP, LUMP), :] = weighted(m * LUMP, (1 - x_lo) * 512).astype(BF16)
        sum_copy(m).start()
        return carry

    lax.fori_loop(0, LUMPS, partner_half, 0)

    for r in range(8):
        count_src[r : r + 1, :] = to_row(count[pl.ds(r * 128, 128), :])
    count_copy.start()

    def own_half(m, carry):
        own_sum[pl.ds(m * LUMP, LUMP), :] = weighted(m * LUMP, x_lo * 512)
        return carry

    lax.fori_loop(0, LUMPS, own_half, 0)

    def sq_copy(m):
        return remote(sq_src.at[m], sq_dst.at[m], sq_send.at[m], sq_recv.at[m], x_pair)

    def out_copies(m):
        at = pl.ds(m * LUMP, LUMP)
        place = pl.ds(core * 1024 + m * LUMP, LUMP)
        local = pltpu.make_async_copy(
            final.at[at, pl.ds(pl.multiple_of(core * 256, 256), 256)], out_hbm.at[place], out_sem.at[m]
        )
        away = remote(
            final.at[at, pl.ds(pl.multiple_of(other * 256, 256), 256)],
            out_hbm.at[place],
            out_send.at[m],
            out_recv.at[m],
            sibling,
        )
        return local, away

    def finish(m):
        at = pl.ds(m * LUMP, LUMP)
        sum_copy(m).wait_recv()
        total = own_sum[at, :] + sum_recv[at, :].astype(F32)
        own_sum[at, :] = total
        squares = total * total
        lanes = squares[:, :128] + squares[:, 128:256] + squares[:, 256:384] + squares[:, 384:]
        sq_src[m] = jnp.concatenate(
            [to_row(lanes[i * 128 : (i + 1) * 128]) for i in range(LUMP // 128)]
            + [jnp.zeros((8 - LUMP // 128, 128), F32)],
            axis=0,
        )
        sq_copy(m).start()

    def normalize(m):
        sq_copy(m).wait_recv()
        for i in range(LUMP // 128):
            at = pl.ds(m * LUMP + i * 128, 128)
            squares = sq_src[m, i : i + 1, :] + sq_dst[m, i : i + 1, :]
            factor = jnp.broadcast_to(lax.rsqrt(squares + 1e-06), (128, 128)).T
            for tile in range(4):
                lanes = pl.ds(tile * 128, 128)
                final[at, lanes] = (own_sum[at, lanes] * factor).astype(BF16)
        local, away = out_copies(m)
        local.start()
        away.start()

    def last(m, carry):
        pl.when(m < LUMPS)(lambda: finish(m))
        pl.when(m > 0)(lambda: normalize(m - 1))
        return carry

    lax.fori_loop(0, LUMPS + 1, last, 0)

    count_copy.wait_recv()
    mine = pl.ds(pl.multiple_of(core * 8, 8), 8)
    count_all[mine, :] = count_src[...] + count_dst[...]
    all_copy = remote(count_all.at[mine], count_all.at[mine], all_send, all_recv, sibling)
    all_copy.start()

    pre.wait_send()
    wait_bytes(rows.at[pl.ds(0, (SLOTS - 1) * 2 * HALF)], row_send)
    wait_bytes(rows.at[pl.ds(0, SLOTS * NODE)], sib_send)
    wait_bytes(rows.at[pl.ds(0, SLOTS * (OWN - EARLY))], late_send)
    wait_bytes(part_dst.at[pl.ds(1, 4 * SLOTS - 1)], part_send)
    wait_bytes(inv.at[pl.ds(1, 2 * SLOTS - 1)], inv_send)
    count_copy.wait_send()
    for m in range(LUMPS):
        sum_copy(m).wait_send()
        sq_copy(m).wait_send()
        local, away = out_copies(m)
        local.wait()
        away.wait()
    all_copy.wait()
    count_out[...] = count_all[...]


def place_results(new_ref, count_ref, log_ref, new_out, count_out, log_out):
    new_out[...] = new_ref[...]
    count_out[...] = count_ref[...]
    log_out[...] = log_ref[:, :OWN]


def on_device(embeddings, centroids):
    dma = pltpu.SemaphoreType.DMA
    any_space = pl.BlockSpec(memory_space=pl.ANY)
    vmem = pl.BlockSpec(memory_space=pltpu.VMEM)
    quarter = pl.BlockSpec((512, 256), lambda i: (i, 0))

    def whole(*shape):
        return pl.BlockSpec(shape, lambda i: (0, 0))

    new_centroids, counts, logs = pl.pallas_call(
        kernel,
        out_shape=(
            jax.ShapeDtypeStruct((2048, 256), BF16),
            jax.ShapeDtypeStruct((16, 128), F32),
            jax.ShapeDtypeStruct((1, 128), F32),
        ),
        in_specs=[any_space, any_space],
        out_specs=(any_space, vmem, vmem),
        scratch_shapes=[
            pltpu.VMEM((ROWS, 1024), BF16),
            pltpu.VMEM((1024, ROWS), BF16),
            pltpu.VMEM((1024, 1024), BF16),
            pltpu.VMEM((OWN, 1024), BF16),
            pltpu.VMEM((1024, 512), F32),
            pltpu.VMEM((1024, 512), BF16),
            pltpu.VMEM((1024, 512), BF16),
            pltpu.VMEM((1024, 512), BF16),
            pltpu.VMEM((2 * SLOTS, 1, PART), F32),
            pltpu.VMEM((4 * SLOTS, 1, PART), F32),
            pltpu.VMEM((2 * SLOTS, 1, PART), F32),
            pltpu.VMEM((1, PART), F32),
            pltpu.VMEM((1, ROWS), F32),
            pltpu.VMEM((1024, 128), F32),
            pltpu.VMEM((8, 128), F32),
            pltpu.VMEM((8, 128), F32),
            pltpu.VMEM((16, 128), F32),
            pltpu.VMEM((LUMPS, 8, 128), F32),
            pltpu.VMEM((LUMPS, 8, 128), F32),
            dma((2,)),
            dma, dma((SLOTS, 2)),
            dma, dma((SLOTS, 2)),
            dma, dma,
            dma, dma((SLOTS,)),
            dma, dma,
            dma, dma,
            dma((LUMPS,)), dma((LUMPS,)),
            dma, dma,
            dma((LUMPS,)), dma((LUMPS,)),
            dma((LUMPS,)), dma((LUMPS,)), dma((LUMPS,)),
            dma, dma,
        ],
        compiler_params=pltpu.CompilerParams(
            collective_id=0, has_side_effects=True, vmem_limit_bytes=60 * 1024 * 1024
        ),
        name="soft_kmeans",
    )(embeddings, centroids)
    new_centroids, counts, logs = pl.pallas_call(
        place_results,
        out_shape=(
            jax.ShapeDtypeStruct((2048, 256), BF16),
            jax.ShapeDtypeStruct((16, 128), F32),
            jax.ShapeDtypeStruct((1, OWN), F32),
        ),
        grid=(4,),
        in_specs=[quarter, whole(16, 128), whole(1, 128)],
        out_specs=(quarter, whole(16, 128), whole(1, OWN)),
        name="place_results",
    )(new_centroids, counts, logs)
    return new_centroids, counts.reshape(2048), logs.reshape(OWN)


def solution(mesh):
    return jax.shard_map(
        on_device,
        mesh=mesh,
        in_specs=(P(("dp", "comp"), None), P("comp", None)),
        out_specs=(P("comp", "dp"), P("comp"), P(("dp", "comp"))),
        check_vma=False,
    )
```

time: 720 us -> 110 us (0.15)
  blocking collectives: 367 us -> 0 us
  waiting for transfers between devices: 239 us -> 0 us
  Pallas kernels: 0 us -> 109 us
  matrix products: 68.2 us -> 0 us
  other arithmetic: 30.9 us -> 0 us
  between operations: 14.1 us -> 0.64 us
    psum x5 -> x0, blocking collectives: 367 us -> none  [the longest x4 305 us: block_step(): totals = lax.psum(jnp.sum(probs, axis=1), 'comp')]
    psum x1 -> x0, waiting for transfers between devices: 149 us -> none  [on_device(): weighted_all, counts_all = lax.psum((weighted, counts), 'dp')]
    pallas_call x0 -> x2, Pallas kernels: none -> 109 us  [the longest x1 106 us: on_device(): pl.pallas_call(kernel, out_shape=(jax.ShapeDtypeStruct((2048, 256), BF16)...]
    all_gather x1 -> x0, waiting for transfers between devices: 90 us -> none  [on_device(): lax.all_gather(unit_rows(embeddings), 'comp', axis=0, tiled=True)]
    dot_general x8 -> x0, matrix products: 68.2 us -> none  [the longest x4 35.7 us: probabilities(): lax.dot_general(row_block, centroid_unit, (((1,), (1,)), ((), ())), prefe...]
    reduce_sum x7 -> x0, other arithmetic: 23 us -> none  [the longest x4 14.7 us: accumulate(): counts = counts + jnp.sum(weights.astype(jnp.float32), axis=0)]
    convert_element_type x3 -> x0, other arithmetic: 7.33 us -> none  [the longest x2 4.42 us: unit_rows(): (floats * lax.rsqrt(jnp.sum(floats * floats, axis=1, keepdims=True) + 1e-...]
  transfers between devices with their start and end apart: 2 -> 0, of which waited for: 2 -> 0; matrix products, arithmetic and copies ran while one was open for 1% -> 0% of each run, Pallas kernels for 0% -> 0%
where the time goes in v2:
time: 110 us
  Pallas kernels  109 us (99%)
    pallas_call x1, Pallas kernels, on_device(): pl.pallas_call(kernel, out_shape=(jax.ShapeDtypeStruct((2048, 256), BF16)...  106 us
    pallas_call x1, Pallas kernels, on_device(): pl.pallas_call(place_results, out_shape=(jax.ShapeDtypeStruct((2048, 256)...  3.38 us

profile of v2, /device:TPU:1, one launch (start us, length us, event | category | flops | bytes accessed | tf_op | source)
XLA Modules:
  0.0 109.8 jit_solution(18169869724650483968)
XLA Ops:
  0.6 105.8 %soft_kmeans.1 = (bf16[2048,256]{1,0:T(8,128)(2,1)}, f32[16,128]{1,0:T(8,128)}, f32[1,128]{1,0:T(1,128)}) custom-call(bf16[96,1024]{1,0:T(8,128)(2,1)} %emb_hbm.1, bf16[2048,1024]{1,0:T(8,128)(2,1)} %cent_hbm.1), custom_call_target="tpu_custom_call" | custom-call | tf_op jit(solution)/shard_map/soft_kmeans/pallas_call | solution.py:393
  106.5 3.4 %place_results.1 = (bf16[2048,256]{1,0:T(8,128)(2,1)}, f32[16,128]{1,0:T(8,128)}, f32[1,96]{1,0:T(1,128)}) custom-call(bf16[2048,256]{1,0:T(8,128)(2,1)} %get-tuple-element.9.new_ref, f32[16,128]{1,0:T(8,128)} %get-tuple-element.10.count_ref, f32[1,128]{1,0:T(1,128)} %get-tuple-element.11.log_ref), custom_call_target="tpu_custom_call" | custom-call | tf_op jit(solution)/shard_map/place_results/pallas_call | solution.py:440

commit v3 on v2

--- a/solution.py
+++ b/solution.py
@@ -18,10 +18,10 @@
 OWN = 96
 EARLY = 64
 NODE = 2 * OWN
-HALF = (OWN + EARLY) // 2
+HALVES = ((0, OWN), (OWN, EARLY))
 STEP = 2 * NODE
 ROWS = SLOTS * STEP
-LEAD = 2
+LEAD = 3
 PART = 256
 LUMP = 256
 LUMPS = 1024 // LUMP
@@ -75,13 +75,15 @@
 
     at_y = [lax.rem(y + sign * d + 4, 4) for d in range(4)]
     at_z = [lax.rem(z + sign * d + 4, 4) * 8 for d in range(4)]
+    at_first = [y_id * other + z_id * core for y_id, z_id in zip(at_y, at_z)]
+    at_second = [y_id * core + z_id * other for y_id, z_id in zip(at_y, at_z)]
     at_x = [lax.rem(x + d, 4) for d in range(4)]
     at_x_comp = [(place // 2) * 4 for place in at_x]
     at_x_dp = [lax.rem(place, 2) * 2 for place in at_x]
     cores = (core, other)
 
-    def device(dx, dy, dz, dcore):
-        comp_id = at_z[dz % 4] + at_x_comp[dx % 4] + at_y[dy % 4]
+    def device(dx, first, second, dcore):
+        comp_id = at_first[first % 4] + at_x_comp[dx % 4] + at_second[second % 4]
         return {"dp": at_x_dp[dx % 4] + cores[dcore], "comp": comp_id}
 
     def remote(src, dst, ssem, rsem, target):
@@ -96,24 +98,24 @@
     x_far = device(2, 0, 0, 0)
     x_pair = {"dp": (1 - x_lo) * 2 + core, "comp": comp}
 
+    emb_copy = pltpu.make_async_copy(emb_hbm, emb, load_sem.at[0])
+    emb_copy.start()
+    cent_copy = pltpu.make_async_copy(cent_hbm.at[pl.ds(core * 1024, 1024)], cent, load_sem.at[1])
+    cent_copy.start()
+
     barrier = pltpu.get_barrier_semaphore()
     greeted = 0
-    for dy, dz in ORDER:
+    for place in ORDER:
         for dcore in (0, 1):
-            if (dy, dz, dcore) != (0, 0, 0):
-                pl.semaphore_signal(barrier, inc=1, device_id=device(0, dy, dz, dcore), device_id_type=MESH)
+            if (*place, dcore) != (0, 0, 0):
+                pl.semaphore_signal(barrier, inc=1, device_id=device(0, *place, dcore), device_id_type=MESH)
                 greeted += 1
-            pl.semaphore_signal(barrier, inc=1, device_id=device(2, dy, dz, dcore), device_id_type=MESH)
+            pl.semaphore_signal(barrier, inc=1, device_id=device(2, *place, dcore), device_id_type=MESH)
             greeted += 1
     for dx in (1, 3):
         pl.semaphore_signal(barrier, inc=1, device_id=device(dx, 0, 0, 0), device_id_type=MESH)
         greeted += 1
 
-    emb_copy = pltpu.make_async_copy(emb_hbm, emb, load_sem.at[0])
-    emb_copy.start()
-    cent_copy = pltpu.make_async_copy(cent_hbm.at[pl.ds(core * 1024, 1024)], cent, load_sem.at[1])
-    cent_copy.start()
-
     def unit(values):
         floats = values.astype(F32)
         return (floats * lax.rsqrt(jnp.sum(floats * floats, axis=1, keepdims=True) + 1e-06)).astype(BF16)
@@ -126,13 +128,14 @@
     pre.start()
 
     def row_copy(slot, half, child, axis, way):
-        dy, dz = (way, 0) if axis == 0 else (0, way)
+        first, second = (way, 0) if axis == 0 else (0, way)
+        start, size = HALVES[half]
         return remote(
-            rows.at[pl.ds(slot * STEP + half * HALF, HALF)],
-            rows.at[pl.ds(child * STEP + half * HALF, HALF)],
+            rows.at[pl.ds(slot * STEP + start, size)],
+            rows.at[pl.ds(child * STEP + start, size)],
             row_send,
             row_recv.at[child, half],
-            device(0, dy, dz, 0),
+            device(0, first, second, 0),
         )
 
     def hand_on(slot, half):
@@ -157,10 +160,11 @@
         )
 
     def arrive(slot):
-        for half in (0, 1):
-            row_copy(slot, half, slot, 0, 1).wait_recv()
-            hand_on(slot, half)
+        row_copy(slot, 0, slot, 0, 1).wait_recv()
+        hand_on(slot, 0)
         late_copy(slot).start()
+        row_copy(slot, 1, slot, 0, 1).wait_recv()
+        hand_on(slot, 1)
         to_sibling(slot, 0).start()
 
     hand_on(0, 0)
@@ -189,16 +193,15 @@
             part_src[2 * (slot - 1 + i) + 1] = pltpu.roll(node, STEP - NODE, 1)[:, :PART]
 
     def send_part(slot):
-        dy, dz = ORDER[slot]
-        for dcore, way in ((0, -1), (1, 1)):
+        first, second = ORDER[slot]
+        for dcore, place in ((0, (-first, -second)), (1, (second, first))):
             tile = 2 * slot + dcore
-            for dx, first in ((0, 0), (2, 2 * SLOTS)):
+            for dx, base in ((0, 0), (2, 2 * SLOTS)):
                 if dx + tile == 0:
                     part_dst[0] = part_src[0]
                 else:
                     remote(
-                        part_src.at[tile], part_dst.at[first + tile], part_send, part_recv,
-                        device(dx, way * dy, way * dz, dcore),
+                        part_src.at[tile], part_dst.at[base + tile], part_send, part_recv, device(dx, *place, dcore)
                     ).start()
 
     def totals_first():
@@ -210,11 +213,11 @@
         total = jnp.where(lane < NODE, total, 1.0)
         inv_src[...] = 1.0 / total
         inv[0] = 1.0 / total
-        for slot, (dy, dz) in enumerate(ORDER):
+        for slot, place in enumerate(ORDER):
             for dcore in (0, 1):
                 if slot + dcore > 0:
                     remote(
-                        inv_src, inv.at[2 * slot + dcore], inv_send, inv_recv, device(0, dy, dz, dcore)
+                        inv_src, inv.at[2 * slot + dcore], inv_send, inv_recv, device(0, *place, dcore)
                     ).start()
         log_out[...] = jnp.log(total[:, :128]) + 10.0
 
@@ -359,7 +362,7 @@
     all_copy.start()
 
     pre.wait_send()
-    wait_bytes(rows.at[pl.ds(0, (SLOTS - 1) * 2 * HALF)], row_send)
+    wait_bytes(rows.at[pl.ds(0, (SLOTS - 1) * (OWN + EARLY))], row_send)
     wait_bytes(rows.at[pl.ds(0, SLOTS * NODE)], sib_send)
     wait_bytes(rows.at[pl.ds(0, SLOTS * (OWN - EARLY))], late_send)
     wait_bytes(part_dst.at[pl.ds(1, 4 * SLOTS - 1)], part_send)

time: 110 us -> 106 us (0.964)
  Pallas kernels: 109 us -> 105 us
    pallas_call x1, Pallas kernels: 106 us -> 101 us  [on_device(): pl.pallas_call(kernel, out_shape=(jax.ShapeDtypeStruct((2048, 256), BF16)...]
where the time goes in v3:
time: 106 us; the launch traced here: 105 us
  Pallas kernels  105 us (99%)
    pallas_call x1, Pallas kernels, on_device(): pl.pallas_call(kernel, out_shape=(jax.ShapeDtypeStruct((2048, 256), BF16)...  101 us
    pallas_call x1, Pallas kernels, on_device(): pl.pallas_call(place_results, out_shape=(jax.ShapeDtypeStruct((2048, 256)...  3.38 us

profile of v3, /device:TPU:1, one launch (start us, length us, event | category | flops | bytes accessed | tf_op | source)
XLA Modules:
  0.0 105.4 jit_solution(14048943385246738001)
XLA Ops:
  0.6 101.3 %soft_kmeans.1 = (bf16[2048,256]{1,0:T(8,128)(2,1)}, f32[16,128]{1,0:T(8,128)}, f32[1,128]{1,0:T(1,128)}) custom-call(bf16[96,1024]{1,0:T(8,128)(2,1)} %emb_hbm.1, bf16[2048,1024]{1,0:T(8,128)(2,1)} %cent_hbm.1), custom_call_target="tpu_custom_call" | custom-call | tf_op jit(solution)/shard_map/soft_kmeans/pallas_call | solution.py:396
  102.0 3.4 %place_results.1 = (bf16[2048,256]{1,0:T(8,128)(2,1)}, f32[16,128]{1,0:T(8,128)}, f32[1,96]{1,0:T(1,128)}) custom-call(bf16[2048,256]{1,0:T(8,128)(2,1)} %get-tuple-element.9.new_ref, f32[16,128]{1,0:T(8,128)} %get-tuple-element.10.count_ref, f32[1,128]{1,0:T(1,128)} %get-tuple-element.11.log_ref), custom_call_target="tpu_custom_call" | custom-call | tf_op jit(solution)/shard_map/place_results/pallas_call | solution.py:443

commit v4 on v3

--- a/solution.py
+++ b/solution.py
@@ -167,6 +167,10 @@
         hand_on(slot, 1)
         to_sibling(slot, 0).start()
 
+    def arrive_late(slot):
+        late_copy(slot).wait_recv()
+        to_sibling(slot, 1).start()
+
     hand_on(0, 0)
     pre.wait_recv()
     hand_on(0, 1)
@@ -213,7 +217,8 @@
         total = jnp.where(lane < NODE, total, 1.0)
         inv_src[...] = 1.0 / total
         inv[0] = 1.0 / total
-        for slot, place in enumerate(ORDER):
+        for slot in reversed(range(SLOTS)):
+            place = ORDER[slot]
             for dcore in (0, 1):
                 if slot + dcore > 0:
                     remote(
@@ -266,8 +271,9 @@
         def _():
             choose(t + LEAD, LEAD, SLOTS, arrive)
 
-        late_copy(t).wait_recv()
-        to_sibling(t, 1).start()
+        @pl.when(t < SLOTS - 1)
+        def _():
+            arrive_late(t + 1)
 
         @pl.when(lax.rem(t, 2) == 1)
         def _():
@@ -281,6 +287,7 @@
 
     for slot in range(1, LEAD):
         arrive(slot)
+    arrive_late(0)
     lax.fori_loop(0, SLOTS, step, 0)
     totals_first()
     totals_second()

time: 106 us -> 103 us (0.972)
  Pallas kernels: 105 us -> 102 us
    pallas_call x1, Pallas kernels: 101 us -> 99.1 us  [on_device(): pl.pallas_call(kernel, out_shape=(jax.ShapeDtypeStruct((2048, 256), BF16)...]
where the time goes in v4:
time: 103 us
  Pallas kernels  102 us (99%)
    pallas_call x1, Pallas kernels, on_device(): pl.pallas_call(kernel, out_shape=(jax.ShapeDtypeStruct((2048, 256), BF16)...  99.1 us
    pallas_call x1, Pallas kernels, on_device(): pl.pallas_call(place_results, out_shape=(jax.ShapeDtypeStruct((2048, 256)...  3.38 us

profile of v4, /device:TPU:1, one launch (start us, length us, event | category | flops | bytes accessed | tf_op | source)
XLA Modules:
  0.0 103.1 jit_solution(6806050289665412768)
XLA Ops:
  0.6 99.1 %soft_kmeans.1 = (bf16[2048,256]{1,0:T(8,128)(2,1)}, f32[16,128]{1,0:T(8,128)}, f32[1,128]{1,0:T(1,128)}) custom-call(bf16[96,1024]{1,0:T(8,128)(2,1)} %emb_hbm.1, bf16[2048,1024]{1,0:T(8,128)(2,1)} %cent_hbm.1), custom_call_target="tpu_custom_call" | custom-call | tf_op jit(solution)/shard_map/soft_kmeans/pallas_call | solution.py:403
  99.7 3.4 %place_results.1 = (bf16[2048,256]{1,0:T(8,128)(2,1)}, f32[16,128]{1,0:T(8,128)}, f32[1,96]{1,0:T(1,128)}) custom-call(bf16[2048,256]{1,0:T(8,128)(2,1)} %get-tuple-element.9.new_ref, f32[16,128]{1,0:T(8,128)} %get-tuple-element.10.count_ref, f32[1,128]{1,0:T(1,128)} %get-tuple-element.11.log_ref), custom_call_target="tpu_custom_call" | custom-call | tf_op jit(solution)/shard_map/place_results/pallas_call | solution.py:450

commit v5 on v4

--- a/solution.py
+++ b/solution.py
@@ -252,9 +252,9 @@
     def to_row(block):
         return jnp.sum(block.T, axis=0, keepdims=True)
 
-    def weighted(start, column):
+    def weighted(start, column, size=LUMP):
         return lax.dot_general(
-            probs[pl.ds(start, LUMP), :],
+            probs[pl.ds(start, size), :],
             rows[:, pl.ds(column, 512)],
             (((1,), (0,)), ((), ())),
             preferred_element_type=F32,
@@ -292,13 +292,22 @@
     totals_first()
     totals_second()
 
+    def partner_sums(start, size, m):
+        at = pl.ds(start, size)
+        scale(start, size)
+        sum_send[at, :] = weighted(start, (1 - x_lo) * 512, size).astype(BF16)
+        remote(sum_send.at[at], sum_recv.at[at], sum_ssem.at[m], sum_rsem.at[m], x_pair).start()
+
+    def first_lump(i, carry):
+        partner_sums(i * (LUMP // 2), LUMP // 2, 0)
+        return carry
+
     def partner_half(m, carry):
-        scale(m * LUMP, LUMP)
-        sum_send[pl.ds(m * LUMP, LUMP), :] = weighted(m * LUMP, (1 - x_lo) * 512).astype(BF16)
-        sum_copy(m).start()
-        return carry
-
-    lax.fori_loop(0, LUMPS, partner_half, 0)
+        partner_sums(m * LUMP, LUMP, m)
+        return carry
+
+    lax.fori_loop(0, 2, first_lump, 0)
+    lax.fori_loop(1, LUMPS, partner_half, 0)
 
     for r in range(8):
         count_src[r : r + 1, :] = to_row(count[pl.ds(r * 128, 128), :])

time: 103 us -> 102 us (level)
    pallas_call x1, Pallas kernels: 99.1 us -> 97.7 us  [on_device(): pl.pallas_call(kernel, out_shape=(jax.ShapeDtypeStruct((2048, 256), BF16)...]
where the time goes in v5:
time: 102 us
  Pallas kernels  101 us (99%)
    pallas_call x1, Pallas kernels, on_device(): pl.pallas_call(kernel, out_shape=(jax.ShapeDtypeStruct((2048, 256), BF16)...  97.7 us
    pallas_call x1, Pallas kernels, on_device(): pl.pallas_call(place_results, out_shape=(jax.ShapeDtypeStruct((2048, 256)...  3.38 us

profile of v5, /device:TPU:1, one launch (start us, length us, event | category | flops | bytes accessed | tf_op | source)
XLA Modules:
  0.0 101.7 jit_solution(12778209006466225881)
XLA Ops:
  0.6 97.7 %soft_kmeans.1 = (bf16[2048,256]{1,0:T(8,128)(2,1)}, f32[16,128]{1,0:T(8,128)}, f32[1,128]{1,0:T(1,128)}) custom-call(bf16[96,1024]{1,0:T(8,128)(2,1)} %emb_hbm.1, bf16[2048,1024]{1,0:T(8,128)(2,1)} %cent_hbm.1), custom_call_target="tpu_custom_call" | custom-call | tf_op jit(solution)/shard_map/soft_kmeans/pallas_call | solution.py:412
  98.3 3.4 %place_results.1 = (bf16[2048,256]{1,0:T(8,128)(2,1)}, f32[16,128]{1,0:T(8,128)}, f32[1,96]{1,0:T(1,128)}) custom-call(bf16[2048,256]{1,0:T(8,128)(2,1)} %get-tuple-element.9.new_ref, f32[16,128]{1,0:T(8,128)} %get-tuple-element.10.count_ref, f32[1,128]{1,0:T(1,128)} %get-tuple-element.11.log_ref), custom_call_target="tpu_custom_call" | custom-call | tf_op jit(solution)/shard_map/place_results/pallas_call | solution.py:459
